TPU v7x, 256 devices: a whole 4x4x8 slice. The times are simulated.
256 devices in a mesh: dom: 64 (over y, z, x_lo), rep: 4 (over x_hi, core).
Axes of the slice: x: 4 (x_hi: 2, x_lo: 2; x = x_hi * 2 + x_lo), y: 4, z: 8, core: 2. Of those that a mesh axis runs over, the one named last changes fastest.
Arguments:
- entity_table: bfloat16 [200, 32768], P(None, ('dom', 'rep')), may hold values from -1.5 to 1.5
- relation_diag: bfloat16 [200, 2176], replicated, may hold values from -4 to 4
- plan: int32 [4], replicated, may hold values from 1 to 63, as said below
- edge_count: int32 [4, 64], replicated, may hold values from 1025 to 4096, as said below
- src_rows: int32 [4, 262144], P(None, ('dom', 'rep')), may hold values from 0 to 511
- dst_rows: int32 [4, 262144], P(None, ('dom', 'rep')), may hold values from 0 to 511
- rel_ids: int32 [4, 262144], P(None, ('dom', 'rep')), may hold values from 0 to 2175
- neg_rows: int32 [4, 1024, 1024], P(None, ('dom', 'rep')), may hold values from 0 to 511
Outputs:
- entity_grad: float32 [200, 32768], P(None, ('dom', 'rep'))
- relation_grad: float32 [200, 2176], replicated
Inputs may be any that keep to these rules, and one draw needn't show every extreme that they name: `plan`: the offsets of the 4 rounds are distinct, and 1, 32 and 63 are among them. `edge_count`: in every round one bucket is full.
All inputs are finite; a program needn't handle non-finite values.
Results may differ from a plain program's by a relative error of at most 0.002.
Values may be sent and summed in bfloat16 or wider, within the bound.
No kernel may reach another device: no remote copies, remote signals or barrier semaphores. Data moves between devices by JAX's collectives and lax.ppermute only.
A program may use at most 64 MiB of HBM per device.

v0:
```python
import jax
import jax.numpy as jnp
from jax import lax
from jax.sharding import PartitionSpec as P


def from_behind(value, axis, steps):
    count = lax.axis_size(axis)
    pairs = [(source, (source + steps) % count) for source in range(count)]
    return lax.ppermute(value, axis, pairs)


def block_grads(src_part, dst_part, relation_diag, src_idx, dst_idx, rel_idx, neg_idx, live):
    src_emb = jnp.take(src_part, src_idx, axis=1)
    dst_emb = jnp.take(dst_part, dst_idx, axis=1)
    neg_emb = jnp.take(dst_part, neg_idx, axis=1)
    rel_emb = jnp.take(relation_diag, rel_idx, axis=1)
    rel_wide = rel_emb.astype(jnp.float32)
    src_wide = src_emb.astype(jnp.float32)
    lhs = (src_wide * rel_wide).astype(jnp.bfloat16)
    lhs_wide = lhs.astype(jnp.float32)
    positive = jnp.sum(lhs_wide * dst_emb.astype(jnp.float32), axis=0)
    negative = jnp.dot(lhs.T, neg_emb, preferred_element_type=jnp.float32)
    pos_weight = -live * jax.nn.sigmoid(-positive)
    neg_weight = (live[:, None] * neg_emb.shape[1] ** (-0.5) * jax.nn.sigmoid(negative)).astype(
        jnp.bfloat16
    )
    grad_lhs = pos_weight[None, :] * dst_emb.astype(jnp.float32) + jnp.dot(
        neg_emb, neg_weight.T, preferred_element_type=jnp.float32
    )
    grad_neg = jnp.dot(lhs, neg_weight, preferred_element_type=jnp.float32)
    return (
        (grad_lhs * rel_wide).astype(jnp.bfloat16),
        (grad_lhs * src_wide).astype(jnp.bfloat16),
        (pos_weight[None, :] * lhs_wide).astype(jnp.bfloat16),
        grad_neg.astype(jnp.bfloat16),
    )


def one_hot_rows(indices, width):
    columns = jnp.arange(width, dtype=jnp.int32)
    return (indices[:, None] == columns[None, :]).astype(jnp.bfloat16)


def add_block(src_acc, dst_acc, rel_acc, terms, src_idx, dst_idx, rel_idx, neg_idx):
    grad_src, grad_rel, grad_dst, grad_neg = terms
    part_rows = src_acc.shape[1]
    src_acc = src_acc + jnp.dot(
        grad_src, one_hot_rows(src_idx, part_rows), preferred_element_type=jnp.float32
    )
    dst_acc = dst_acc + jnp.dot(
        grad_dst, one_hot_rows(dst_idx, part_rows), preferred_element_type=jnp.float32
    )
    dst_acc = dst_acc + jnp.dot(
        grad_neg, one_hot_rows(neg_idx, part_rows), preferred_element_type=jnp.float32
    )
    rel_acc = rel_acc + jnp.dot(
        grad_rel, one_hot_rows(rel_idx, rel_acc.shape[1]), preferred_element_type=jnp.float32
    )
    return (src_acc, dst_acc, rel_acc)


def per_device(
    entity_table, relation_diag, plan, edge_count, src_rows, dst_rows, rel_ids, neg_rows
):
    n_dom = lax.axis_size("dom")
    n_rep = lax.axis_size("rep")
    dom_index = lax.axis_index("dom")
    rep_index = lax.axis_index("rep")
    rounds = plan.shape[0]
    blocks_dev = neg_rows.shape[1]
    span = src_rows.shape[1] // blocks_dev
    width = entity_table.shape[0]
    quarter = entity_table.shape[1]
    part_rows = quarter * n_rep
    hops = (n_dom - 1).bit_length()
    src_part = lax.all_gather(entity_table, "rep", axis=1, tiled=True)
    src_all = src_rows.reshape(rounds, blocks_dev, span)
    dst_all = dst_rows.reshape(rounds, blocks_dev, span)
    rel_all = rel_ids.reshape(rounds, blocks_dev, span)
    first_block = rep_index * blocks_dev
    stride = 1
    every_part = lax.all_gather(entity_table, "dom", axis=1, tiled=True)
    src_grad = jnp.zeros((width, part_rows), jnp.float32)
    ent_grad = jnp.zeros((width, quarter), jnp.float32)
    rel_grad = jnp.zeros(relation_diag.shape, jnp.float32)
    rel_total = jnp.zeros(relation_diag.shape, jnp.float32)
    for step in range(rounds):
        offset = plan[step]
        target = (dom_index + offset) % n_dom
        target_quarter = lax.dynamic_slice_in_dim(every_part, target * quarter, quarter, 1)
        dst_part = lax.all_gather(target_quarter, "rep", axis=1, tiled=True)
        count = edge_count[step, dom_index]
        total_blocks = (count + span - 1) // span
        used = jnp.clip((total_blocks - first_block + stride - 1) // stride, 0, blocks_dev)
        src_step = src_all[step]
        dst_step = dst_all[step]
        rel_step = rel_all[step]
        neg_step = neg_rows[step]

        def one_block(block, inner):
            s_acc, d_acc, r_acc = inner
            global_block = first_block + block * stride
            slot = global_block * span + jnp.arange(span, dtype=jnp.int32)
            live = (slot < count).astype(jnp.float32)
            src_idx = src_step[block]
            dst_idx = dst_step[block]
            rel_idx = rel_step[block]
            neg_idx = neg_step[block]
            terms = block_grads(
                src_part, dst_part, relation_diag, src_idx, dst_idx, rel_idx, neg_idx, live
            )
            return add_block(s_acc, d_acc, r_acc, terms, src_idx, dst_idx, rel_idx, neg_idx)

        dst_grad = jnp.zeros((width, part_rows), jnp.float32)
        src_grad, dst_grad, rel_grad = lax.fori_loop(
            0, used, one_block, (src_grad, dst_grad, rel_grad)
        )
        returned = lax.psum_scatter(dst_grad, "rep", scatter_dimension=1, tiled=True)
        for bit in range(hops):
            moved = from_behind(returned, "dom", 1 << bit)
            returned = jnp.where((offset >> bit) % 2 == 1, moved, returned)
        ent_grad = ent_grad + returned
        rel_total = rel_total + lax.psum(rel_grad, ("dom", "rep"))
        rel_grad = jnp.zeros(relation_diag.shape, jnp.float32)
    ent_grad = ent_grad + lax.psum_scatter(src_grad, "rep", scatter_dimension=1, tiled=True)
    return (ent_grad, rel_total)


def solution(mesh):
    in_specs = (
        P(None, ("dom", "rep")),
        P(),
        P(),
        P(),
        P(None, ("dom", "rep")),
        P(None, ("dom", "rep")),
        P(None, ("dom", "rep")),
        P(None, ("dom", "rep"), None),
    )
    out_specs = (P(None, ("dom", "rep")), P())
    return jax.shard_map(
        per_device, mesh=mesh, in_specs=in_specs, out_specs=out_specs, check_vma=False
    )
```

profile of v0, /device:TPU:1, one launch (start us, length us, event | category | flops | bytes accessed | tf_op | source)
XLA Modules:
  0.0 1050.9 jit_solution(692331613105637959)
XLA Ops:
  26.0 10.4 all_gather.18
  36.9 239.6 %all-gather.2.cloned.1.call-done = bf16[200,8192]{0,1:T(8,128)(2,1)} async-done(((bf16[200,128]{0,1:T(8,128)(2,1)}), bf16[200,8192]{0,1:T(8,128)(2,1)}) %all-gather.2.cloned.1.call-update) | async-done | bytes 3276816 | tf_op jit(solution)/shard_map/all_gather | solution.py:83
  278.1 50.0 %all_gather.22 = bf16[200,512]{0,1:T(8,128)(2,1)S(1)} all-gather(bf16[200,128]{0,1:T(8,128)(2,1)S(1)} %get-tuple-element.514), channel_id=1, replica_groups=mesh['dom'=64,'rep'=4] {'rep'}, dimensions={1}, use_global_device_ids=true | all-gather | bytes 256000 | tf_op jit(solution)/shard_map/all_gather | solution.py:92
  328.1 7.4 all_gather.21
  335.5 7.4 all_gather.20
  344.3 22.2 %while.56 = (s32[]{:T(128)}, f32[200,512]{1,0:T(8,128)S(1)}, f32[200,512]{1,0:T(8,128)S(1)}, f32[200,2176]{1,0:T(8,128)}, s32[]{:T(128)}, /*index=5*/s32[]{:T(12...) while((s32[]{:T(128)}, f32[200,512]{1,0:T(8,128)S(1)}, ...), condition=%wide.region_2.6_spmd, body=%wide.region_0.5_spmd.sunk | while | flops 857332224 | bytes 30616372 | solution.py:116
  351.1 5.0 gather_fusion.3
  368.6 22.6 %while.57 = (s32[]{:T(128)}, f32[200,512]{1,0:T(8,128)S(1)}, f32[200,512]{1,0:T(8,128)}, f32[200,2176]{1,0:T(8,128)}, s32[]{:T(128)}, /*index=5*/s32[]{:T(128)},...) while((s32[]{:T(128)}, f32[200,512]{1,0:T(8,128)S(1)}, ...), condition=%wide.region_6.10_spmd, body=%wide.region_4.9_spmd.sunk | while | flops 857332224 | bytes 33034920 | solution.py:116
  376.6 5.0 gather_fusion.7
  392.6 20.1 %while.58 = (s32[]{:T(128)}, f32[200,512]{1,0:T(8,128)S(1)}, f32[200,512]{1,0:T(8,128)S(1)}, f32[200,2176]{1,0:T(8,128)}, s32[]{:T(128)}, /*index=5*/s32[]{:T(12...) while((s32[]{:T(128)}, f32[200,512]{1,0:T(8,128)S(1)}, ...), condition=%wide.region_10.14_spmd, body=%wide.region_8.13_spmd.sunk | while | flops 857332224 | bytes 29758064 | solution.py:116
  399.2 5.0 gather_fusion.11
  414.9 200.1 %all_gather.23 = bf16[200,512]{0,1:T(8,128)(2,1)S(1)} all-gather(bf16[200,128]{0,1:T(8,128)(2,1)S(1)} %copy-done.21), channel_id=1, replica_groups=mesh['dom'=64,'rep'=4] {'rep'}, dimensions={1}, use_global_device_ids=true | all-gather | bytes 256000 | tf_op jit(solution)/shard_map/all_gather | solution.py:92
  616.5 18.3 %while.59 = (s32[]{:T(128)}, f32[200,512]{1,0:T(8,128)S(1)}, f32[200,512]{1,0:T(8,128)S(1)}, f32[200,2176]{1,0:T(8,128)}, s32[]{:T(128)}, /*index=5*/s32[]{:T(12...) while((s32[]{:T(128)}, f32[200,512]{1,0:T(8,128)S(1)}, ...), condition=%wide.region_14.18_spmd, body=%wide.region_12.17_spmd.sunk | while | flops 857332224 | bytes 29758064 | solution.py:116
  621.4 5.0 gather_fusion.15
  648.6 4.6 add_add_fusion
  653.3 15.5 %reduce-scatter.8.cloned.1.call-done = f32[200,128]{1,0:T(8,128)} async-done(((f32[200,512]{1,0:T(8,128)}), f32[200,128]{1,0:T(8,128)}) %reduce-scatter.8.cloned.1.call-update) | async-done | bytes 102416 | tf_op jit(solution)/shard_map/reduce_scatter | solution.py:119
  669.0 34.8 %reduce-scatter.6.cloned.1.call-done = f32[200,128]{1,0:T(8,128)} async-done(((f32[200,512]{1,0:T(8,128)}), f32[200,128]{1,0:T(8,128)}) %reduce-scatter.6.cloned.1.call-update) | async-done | bytes 102416 | tf_op jit(solution)/shard_map/reduce_scatter | solution.py:119
  704.1 36.7 %reduce-scatter.12.cloned.1.call-done = f32[200,128]{1,0:T(8,128)} async-done(((f32[200,512]{1,0:T(8,128)}), f32[200,128]{1,0:T(8,128)}) %reduce-scatter.12.cloned.1.call-update) | async-done | bytes 102416 | tf_op jit(solution)/shard_map/reduce_scatter | solution.py:119
  746.1 3.7 collective-permute-done.18
  774.0 8.7 collective-permute-done.3
  782.8 3.9 collective-permute-done.21
  786.8 5.4 collective-permute-start.17
  792.4 3.0 collective-permute-start.5
  809.1 231.9 %all-reduce.2.cloned.1.call-done = f32[200,2176]{1,0:T(8,128)} async-done(((f32[200,2176]{1,0:T(8,128)}), f32[200,2176]{1,0:T(8,128)}) %all-reduce.2.cloned.1.call-update) | async-done | bytes 1740816 | tf_op jit(solution)/shard_map/psum | solution.py:124
  (298 shorter events, 131.3 us)
Async XLA Ops:
  7.2 269.4 %all-gather.2.cloned.1.call-start = ((), (), s32[]{:S(2)}) async-start(), calls=%async_computation.5 | async-start | bytes 4259840 | tf_op jit(solution)/shard_map/all_gather | solution.py:83
  8.8 639.7 %reduce-scatter.10.cloned.1.call-start = ((), (), s32[]{:S(2)}) async-start(), calls=%async_computation.8 | async-start | bytes 512000 | tf_op jit(solution)/shard_map/reduce_scatter | solution.py:119
  413.4 255.3 %reduce-scatter.8.cloned.1.call-start = ((), (), s32[]{:S(2)}) async-start(), calls=%async_computation.7 | async-start | bytes 512000 | tf_op jit(solution)/shard_map/reduce_scatter | solution.py:119
  414.1 289.7 %reduce-scatter.6.cloned.1.call-start = ((), (), s32[]{:S(2)}) async-start(), calls=%async_computation.6 | async-start | bytes 512000 | tf_op jit(solution)/shard_map/reduce_scatter | solution.py:119
  615.1 125.7 %reduce-scatter.12.cloned.1.call-start = ((), (), s32[]{:S(2)}) async-start(), calls=%async_computation.9 | async-start | bytes 512000 | tf_op jit(solution)/shard_map/reduce_scatter | solution.py:119
  635.7 164.4 %reduce-scatter.14.cloned.1.call-start = ((), (), s32[]{:S(2)}) async-start(), calls=%async_computation.10 | async-start | bytes 512000 | tf_op jit(solution)/shard_map/reduce_scatter | solution.py:126
  648.5 392.6 %all-reduce.2.cloned.1.call-start = ((), (), s32[]{:S(2)}) async-start(), calls=%async_computation.11 | async-start | bytes 3481600 | tf_op jit(solution)/shard_map/psum | solution.py:124
  648.5 92.5 %collective-permute-start.12 = (f32[200,128]{1,0:T(8,128)}, f32[200,128]{1,0:T(8,128)S(1)}, u32[]{:S(2)}, u32[]{:S(2)}) collective-permute-start(f32[200,128]{1,0:T(8,128)} %reduce-scatter.10.cloned.1.call-done), channel_id=1, source_target_pairs={{0,4},{4,8},{8,12},{12,16},{16,20},{20,24},{24,28},{28,32},{32,36}... | collective-permute-start | bytes 307208 | tf_op jit(solution)/shard_map/ppermute | solution.py:10
  668.8 73.7 %collective-permute-start.6 = (f32[200,128]{1,0:T(8,128)}, f32[200,128]{1,0:T(8,128)S(1)}, u32[]{:S(2)}, u32[]{:S(2)}) collective-permute-start(f32[200,128]{1,0:T(8,128)} %reduce-scatter.8.cloned.1.call-done), channel_id=1, source_target_pairs={{0,4},{4,8},{8,12},{12,16},{16,20},{20,24},{24,28},{28,32},{32,36}... | collective-permute-start | bytes 307208 | tf_op jit(solution)/shard_map/ppermute | solution.py:10
  703.8 40.9 %collective-permute-start = (f32[200,128]{1,0:T(8,128)}, f32[200,128]{1,0:T(8,128)S(1)}, u32[]{:S(2)}, u32[]{:S(2)}) collective-permute-start(f32[200,128]{1,0:T(8,128)} %reduce-scatter.6.cloned.1.call-done), channel_id=1, source_target_pairs={{0,4},{4,8},{8,12},{12,16},{16,20},{20,24},{24,28},{28,32},{32,36}... | collective-permute-start | bytes 307208 | tf_op jit(solution)/shard_map/ppermute | solution.py:10
  744.7 10.7 %collective-permute-start.1 = (f32[200,128]{1,0:T(8,128)S(1)}, f32[200,128]{1,0:T(8,128)S(1)}, u32[]{:S(2)}, u32[]{:S(2)}) collective-permute-start(f32[200,128]{1,0:T(8,128)S(1)} %broadcast_select_fusion.47), channel_id=1, source_target_pairs={{0,8},{4,12},{8,16},{12,20},{16,24},{20,28},{24,32},{28,36},{32,40... | collective-permute-start | bytes 307208 | tf_op jit(solution)/shard_map/ppermute | solution.py:10
  753.1 10.0 collective-permute-start.8
  755.5 11.1 %collective-permute-start.2 = (f32[200,128]{1,0:T(8,128)S(1)}, f32[200,128]{1,0:T(8,128)S(1)}, u32[]{:S(2)}, u32[]{:S(2)}) collective-permute-start(f32[200,128]{1,0:T(8,128)S(1)} %broadcast_select_fusion.48), channel_id=1, source_target_pairs={{0,16},{4,20},{8,24},{12,28},{16,32},{20,36},{24,40},{28,44},{32,4... | collective-permute-start | bytes 307208 | tf_op jit(solution)/shard_map/ppermute | solution.py:10
  757.6 11.6 %collective-permute-start.20 = (f32[200,128]{1,0:T(8,128)S(1)}, f32[200,128]{1,0:T(8,128)S(1)}, u32[]{:S(2)}, u32[]{:S(2)}) collective-permute-start(f32[200,128]{1,0:T(8,128)S(1)} %broadcast_select_fusion.33), channel_id=1, source_target_pairs={{0,16},{4,20},{8,24},{12,28},{16,32},{20,36},{24,40},{28,44},{32,4... | collective-permute-start | bytes 307208 | tf_op jit(solution)/shard_map/ppermute | solution.py:10
  758.7 13.1 %collective-permute-start.15 = (f32[200,128]{1,0:T(8,128)S(1)}, f32[200,128]{1,0:T(8,128)S(1)}, u32[]{:S(2)}, u32[]{:S(2)}) collective-permute-start(f32[200,128]{1,0:T(8,128)S(1)} %broadcast_select_fusion.39), channel_id=1, source_target_pairs={{0,32},{4,36},{8,40},{12,44},{16,48},{20,52},{24,56},{28,60},{32,6... | collective-permute-start | bytes 307208 | tf_op jit(solution)/shard_map/ppermute | solution.py:10
  763.1 10.8 %collective-permute-start.9 = (f32[200,128]{1,0:T(8,128)S(1)}, f32[200,128]{1,0:T(8,128)S(1)}, u32[]{:S(2)}, u32[]{:S(2)}) collective-permute-start(f32[200,128]{1,0:T(8,128)S(1)} %broadcast_select_fusion.44), channel_id=1, source_target_pairs={{0,32},{4,36},{8,40},{12,44},{16,48},{20,52},{24,56},{28,60},{32,6... | collective-permute-start | bytes 307208 | tf_op jit(solution)/shard_map/ppermute | solution.py:10
  766.6 16.1 %collective-permute-start.3 = (f32[200,128]{1,0:T(8,128)S(1)}, f32[200,128]{1,0:T(8,128)S(1)}, u32[]{:S(2)}, u32[]{:S(2)}) collective-permute-start(f32[200,128]{1,0:T(8,128)S(1)} %broadcast_select_fusion.49), channel_id=1, source_target_pairs={{0,32},{4,36},{8,40},{12,44},{16,48},{20,52},{24,56},{28,60},{32,6... | collective-permute-start | bytes 307208 | tf_op jit(solution)/shard_map/ppermute | solution.py:10
  769.2 17.4 %collective-permute-start.21 = (f32[200,128]{1,0:T(8,128)S(1)}, f32[200,128]{1,0:T(8,128)S(1)}, u32[]{:S(2)}, u32[]{:S(2)}) collective-permute-start(f32[200,128]{1,0:T(8,128)S(1)} %broadcast_select_fusion.34), channel_id=1, source_target_pairs={{0,32},{4,36},{8,40},{12,44},{16,48},{20,52},{24,56},{28,60},{32,6... | collective-permute-start | bytes 307208 | tf_op jit(solution)/shard_map/ppermute | solution.py:10
  771.8 14.9 %collective-permute-start.16 = (f32[200,128]{1,0:T(8,128)S(1)}, f32[200,128]{1,0:T(8,128)S(1)}, u32[]{:S(2)}, u32[]{:S(2)}) collective-permute-start(f32[200,128]{1,0:T(8,128)S(1)} %broadcast_select_fusion.40), channel_id=1, source_target_pairs={{0,64},{4,68},{8,72},{12,76},{16,80},{20,84},{24,88},{28,92},{32,9... | collective-permute-start | bytes 307208 | tf_op jit(solution)/shard_map/ppermute | solution.py:10
  773.9 18.3 %collective-permute-start.10 = (f32[200,128]{1,0:T(8,128)S(1)}, f32[200,128]{1,0:T(8,128)S(1)}, u32[]{:S(2)}, u32[]{:S(2)}) collective-permute-start(f32[200,128]{1,0:T(8,128)S(1)} %broadcast_select_fusion.45), channel_id=1, source_target_pairs={{0,64},{4,68},{8,72},{12,76},{16,80},{20,84},{24,88},{28,92},{32,9... | collective-permute-start | bytes 307208 | tf_op jit(solution)/shard_map/ppermute | solution.py:10
  786.8 13.5 %collective-permute-start.17 = (f32[200,128]{1,0:T(8,128)S(1)}, f32[200,128]{1,0:T(8,128)S(1)}, u32[]{:S(2)}, u32[]{:S(2)}) collective-permute-start(f32[200,128]{1,0:T(8,128)S(1)} %broadcast_select_fusion.41), channel_id=1, source_target_pairs={{0,128},{4,132},{8,136},{12,140},{16,144},{20,148},{24,152},{28,15... | collective-permute-start | bytes 307208 | tf_op jit(solution)/shard_map/ppermute | solution.py:10
  792.2 10.3 collective-permute-start.11
  792.4 12.7 %collective-permute-start.5 = (f32[200,128]{1,0:T(8,128)S(1)}, f32[200,128]{1,0:T(8,128)S(1)}, u32[]{:S(2)}, u32[]{:S(2)}) collective-permute-start(f32[200,128]{1,0:T(8,128)S(1)} %broadcast_select_fusion.51), channel_id=1, source_target_pairs={{0,128},{4,132},{8,136},{12,140},{16,144},{20,148},{24,152},{28,15... | collective-permute-start | bytes 307208 | tf_op jit(solution)/shard_map/ppermute | solution.py:10
  795.4 12.1 %collective-permute-start.23 = (f32[200,128]{1,0:T(8,128)S(1)}, f32[200,128]{1,0:T(8,128)S(1)}, u32[]{:S(2)}, u32[]{:S(2)}) collective-permute-start(f32[200,128]{1,0:T(8,128)S(1)} %broadcast_select_fusion.36), channel_id=1, source_target_pairs={{0,128},{4,132},{8,136},{12,140},{16,144},{20,148},{24,152},{28,15... | collective-permute-start | bytes 307208 | tf_op jit(solution)/shard_map/ppermute | solution.py:10
  (43 other events, 366.5 us)
Sparse Core Ops, SparseCore 0:
  10.4 266.1 all-gather.1
  413.5 219.9 reduce-scatter.9
  636.3 32.4 reduce-scatter.7
  671.4 32.4 reduce-scatter.5
  706.4 34.3 reduce-scatter.11
  743.4 32.4 reduce-scatter.13
  781.9 259.1 all-reduce.1
where the time goes:
time: 1060 us; the launch traced here: 1050 us
  waiting for transfers between devices  603 us (57%)
  blocking collectives  275 us (26%)
  local copies, waits for them, and re-layouts  78.3 us (7%)
  between operations  35.1 us (3%)
  matrix products  27.2 us (3%)
  starting transfers between devices  19.7 us (2%)
    all_gather x4, blocking collectives, per_device(): dst_part = lax.all_gather(target_quarter, 'rep', axis=1, tiled=True)  265 us
    all_gather x1, waiting for transfers between devices, per_device(): every_part = lax.all_gather(entity_table, 'dom', axis=1, tiled=True)  240 us
    psum x1, waiting for transfers between devices, per_device(): rel_total = rel_total + lax.psum(rel_grad, ('dom', 'rep'))  232 us
    reduce_scatter x4, waiting for transfers between devices, per_device(): lax.psum_scatter(dst_grad, 'rep', scatter_dimension=1, tiled=True)  87 us
    ppermute x24, waiting for transfers between devices, from_behind(): return lax.ppermute(value, axis, pairs)  44 us
  transfers between devices with their start and end apart: 31, of which 21 were waited for; matrix products, arithmetic and copies ran while one was open for 4% of the time, Pallas kernels for 0%

commit v1 on v0

v1 whole, which is shorter than its diff:
```python
import functools

import jax
import jax.numpy as jnp
from jax import lax
from jax.experimental import pallas as pl
from jax.experimental.pallas import tpu as pltpu
from jax.sharding import Mesh, PartitionSpec as P

DOM = ("y", "z", "xl")
REP = ("xh", "core")
CHIPS = ("y", "z", "xl", "xh")
LANES = 128
SPAN = 256
KNOWN = (1, 32, 63)
F32 = jnp.float32
BF16 = jnp.bfloat16


def mm(a, b):
    return jnp.dot(a, b, preferred_element_type=F32)


def mm_nt(a, b):
    return lax.dot_general(a, b, (((1,), (1,)), ((), ())), preferred_element_type=F32)


def one_hot(index, first, height):
    rows = lax.broadcasted_iota(jnp.int32, (height, index.shape[1]), 0) + first
    return jnp.where(rows == index, 1.0, 0.0).astype(BF16)


def rel_chunks(n_rel):
    return [(a, min(2 * LANES, n_rel - a)) for a in range(0, n_rel, 2 * LANES)]


def place(tile, half_tiles):
    return (0, tile) if tile < half_tiles else (1, tile - half_tiles)


def round_kernel(first, half_tiles, meta, src_q, dst_q, rel, srcs, dsts, rels, negs, *rest):
    if first:
        src_o, rel_o, dst_o, hot = rest
        src_o[...] = jnp.zeros_like(src_o)
        rel_o[...] = jnp.zeros_like(rel_o)
    else:
        src_in, rel_in, src_o, rel_o, dst_o, hot = rest
        src_o[...] = src_in[...]
        rel_o[...] = rel_in[...]
    dst_o[...] = jnp.zeros_like(dst_o)
    width, n_rel = rel.shape
    n_q = src_q.shape[0]
    src_t = jnp.concatenate([src_q[q] for q in range(n_q)], axis=1)
    dst_t = jnp.concatenate([dst_q[q] for q in range(n_q)], axis=1)
    dst_wide = dst_t.astype(F32)
    dst_rows = dst_wide.T.astype(BF16)
    part = src_t.shape[1]
    row = meta[0]
    used = meta[1]
    count = meta[2]
    block0 = meta[3]
    stride = meta[4]
    n_neg = negs.shape[2]
    scale = n_neg ** -0.5

    def one_block(k, carry):
        lanes = pl.ds(pl.multiple_of(k * SPAN, SPAN), SPAN)
        src_i = srcs[pl.ds(row, 1), lanes]
        dst_i = dsts[pl.ds(row, 1), lanes]
        rel_i = rels[pl.ds(row, 1), lanes]
        neg_i = negs[row, pl.ds(k, 1), :]
        slot = (block0 + k * stride) * SPAN + lax.broadcasted_iota(jnp.int32, (1, SPAN), 1)
        live = (slot < count).astype(F32)
        src_hot = one_hot(src_i, 0, part)
        dst_hot = one_hot(dst_i, 0, part)
        w = jnp.zeros((width, SPAN), F32)
        for a, n in rel_chunks(n_rel):
            chunk = one_hot(rel_i, a, n)
            hot[a:a + n, :] = chunk
            w = w + mm(rel[:, a:a + n], chunk)
        s = mm(src_t, src_hot)
        t = mm(dst_t, dst_hot)
        lhs = (s * w).astype(BF16)
        lhs_wide = lhs.astype(F32)
        positive = jnp.sum(lhs_wide * t, axis=0, keepdims=True)
        pos_weight = -live * jax.nn.sigmoid(-positive)
        scores = mm(dst_rows, lhs)
        weight = ((live * scale) * jax.nn.sigmoid(scores)).astype(BF16)
        low = one_hot(jnp.bitwise_and(neg_i, LANES - 1), 0, LANES)
        high = one_hot(jnp.right_shift(neg_i, 7), 0, 16)
        times = mm_nt(high, low)
        times = jnp.concatenate([times[q:q + 1, :] for q in range(n_q)], axis=1)
        counted = times * dst_wide
        counted_hi = counted.astype(BF16)
        counted_lo = (counted - counted_hi.astype(F32)).astype(BF16)
        grad_lhs = pos_weight * t + (mm(counted_hi, weight) + mm(counted_lo, weight))
        grad_src = (grad_lhs * w).astype(BF16)
        grad_rel = (grad_lhs * s).astype(BF16)
        grad_dst = (pos_weight * lhs_wide).astype(BF16)
        src_part = mm_nt(grad_src, src_hot)
        grad_neg = mm_nt(lhs, weight).astype(BF16).astype(F32)
        dst_part = mm_nt(grad_dst, dst_hot) + times * grad_neg
        for q in range(n_q):
            cols = slice(q * LANES, (q + 1) * LANES)
            src_o[q] += src_part[:, cols]
            dst_o[q] += dst_part[:, cols]
        for a, n in rel_chunks(n_rel):
            term = mm_nt(grad_rel, hot[a:a + n, :])
            for b in range(n // LANES):
                half, at = place(a // LANES + b, half_tiles)
                rel_o[half, at * width:(at + 1) * width, :] += term[:, b * LANES:(b + 1) * LANES]
        return carry

    lax.fori_loop(0, used, one_block, 0)


def run_round(meta, src_q, dst_q, rel, srcs, dsts, rels, negs, carried):
    n_q, width, lanes = src_q.shape
    n_rel = rel.shape[1]
    half_tiles = -(-(n_rel // LANES) // 2)
    half_rows = -(-half_tiles * width // 2048) * 2048
    vmem = pl.BlockSpec(memory_space=pltpu.VMEM)
    smem = pl.BlockSpec(memory_space=pltpu.SMEM)
    part = jax.ShapeDtypeStruct((n_q, width, lanes), F32)
    ops = [meta, src_q, dst_q, rel, srcs, dsts, rels, negs] + list(carried)
    return pl.pallas_call(
        functools.partial(round_kernel, not carried, half_tiles),
        out_shape=(part, jax.ShapeDtypeStruct((2, half_rows, LANES), F32), part),
        in_specs=[smem] + [vmem] * (len(ops) - 1),
        out_specs=(vmem, vmem, vmem),
        scratch_shapes=[pltpu.VMEM((n_rel, SPAN), BF16)],
        compiler_params=pltpu.CompilerParams(vmem_limit_bytes=48 * 1024 * 1024),
        name="bucket_round",
    )(*ops)


def join_kernel(half_tiles, core, mine, other, out):
    width = out.shape[0]
    n_tiles = out.shape[1] // LANES

    def put(halves):
        for tile in range(n_tiles):
            half, at = place(tile, half_tiles)
            out[:, tile * LANES:(tile + 1) * LANES] = halves[half][at * width:(at + 1) * width, :]

    @pl.when(core[0] == 0)
    def _():
        put((mine, other))

    @pl.when(core[0] != 0)
    def _():
        put((other, mine))


def join_relations(core, mine, other, shape):
    half_tiles = -(-(shape[1] // LANES) // 2)
    vmem = pl.BlockSpec(memory_space=pltpu.VMEM)
    smem = pl.BlockSpec(memory_space=pltpu.SMEM)
    return pl.pallas_call(
        functools.partial(join_kernel, half_tiles),
        out_shape=jax.ShapeDtypeStruct(shape, F32),
        in_specs=[smem, vmem, vmem],
        out_specs=vmem,
        compiler_params=pltpu.CompilerParams(vmem_limit_bytes=24 * 1024 * 1024),
        name="join_relations",
    )(core, mine, other)


def shifted(value, axes, steps):
    count = 1
    for axis in axes:
        count *= lax.axis_size(axis)
    return lax.ppermute(value, axes, [(a, (a + steps) % count) for a in range(count)])


def shifted_by(value, axes, steps):
    for unit in (1, 4, 16):
        digit = (steps // unit) % 4
        moved = [value] + [shifted(value, axes, unit * d) for d in (1, 2, 3)]
        value = jnp.where(
            digit < 2,
            jnp.where(digit == 0, moved[0], moved[1]),
            jnp.where(digit == 2, moved[2], moved[3]),
        )
    return value


def swap(value, axis):
    return lax.ppermute(value, axis, [(0, 1), (1, 0)])


def pick(value, index, axis):
    return lax.dynamic_index_in_dim(value, index, axis, keepdims=False)


def per_device(
    entity_table, relation_diag, plan, edge_count, src_rows, dst_rows, rel_ids, neg_rows
):
    n_dom = 64
    rounds = plan.shape[0]
    blocks_dev = neg_rows.shape[1]
    width, quarter = entity_table.shape
    dom_index = lax.axis_index(DOM)
    rep_index = lax.axis_index(REP)
    core = lax.axis_index("core")
    x_high = lax.axis_index("xh")

    known = jnp.array(KNOWN, jnp.int32)
    is_known = (plan[:, None] == known[None, :]).any(axis=1)
    free_row = jnp.argmin(is_known.astype(jnp.int32)).astype(jnp.int32)
    free_offset = plan[free_row]
    order = [jnp.argmax((plan == k).astype(jnp.int32)).astype(jnp.int32) for k in KNOWN]
    rows = [order[0], order[1], order[2], free_row]

    free_quarter = shifted_by(entity_table, DOM, (n_dom - free_offset) % n_dom)
    src_q = lax.all_gather(entity_table, REP, axis=0, tiled=False)
    dst_parts = [shifted(src_q, DOM, n_dom - k) for k in KNOWN]
    dst_parts.append(lax.all_gather(free_quarter, REP, axis=0, tiled=False))

    first_block = rep_index * blocks_dev
    carried = ()
    returns = []
    for row, dst_q in zip(rows, dst_parts):
        count = edge_count[row, dom_index]
        total = (count + SPAN - 1) // SPAN
        used = jnp.clip(total - first_block, 0, blocks_dev)
        meta = jnp.stack([row, used, count, first_block, jnp.int32(1)]).astype(jnp.int32)
        src_acc, rel_acc, dst_acc = run_round(
            meta, src_q, dst_q, relation_diag, src_rows, dst_rows, rel_ids, neg_rows, carried
        )
        carried = (src_acc, rel_acc)
        returns.append(dst_acc)

    half = pick(rel_acc, core, 0) + swap(pick(rel_acc, 1 - core, 0), "core")
    pieces = lax.all_to_all(half, CHIPS, 0, 0, tiled=True)
    peers = 128
    piece = pieces.reshape(peers, -1, LANES).sum(axis=0)
    whole = lax.all_to_all(jnp.tile(piece, (peers, 1)), CHIPS, 0, 0, tiled=True)
    relation_grad = join_relations(
        core.astype(jnp.int32).reshape(1), whole, swap(whole, "core"), relation_diag.shape
    )

    parts = jnp.stack(returns + [src_acc]).reshape(rounds + 1, 2, 2, width, quarter)
    parts = pick(parts, core, 2) + swap(pick(parts, 1 - core, 2), "core")
    parts = pick(parts, x_high, 1) + swap(pick(parts, 1 - x_high, 1), "xh")
    entity_grad = parts[rounds]
    for at, k in enumerate(KNOWN):
        entity_grad = entity_grad + shifted(parts[at], DOM, k)
    entity_grad = entity_grad + shifted_by(parts[rounds - 1], DOM, free_offset)
    return entity_grad, relation_grad


def solution(mesh):
    fine = Mesh(mesh.devices.reshape(4, 8, 2, 2, 2), DOM + REP)
    cols = P(None, DOM + REP)
    in_specs = (cols, P(), P(), P(), cols, cols, cols, P(None, DOM + REP, None))
    return jax.shard_map(
        per_device, mesh=fine, in_specs=in_specs, out_specs=(cols, P()), check_vma=False
    )
```

time: 1060 us -> 252 us (0.24)
  the two profiles are of different devices: /device:TPU:1 before, /device:TPU:32 now
where the time goes in v1:
time: 252 us; the launch traced here: 251 us
  waiting for transfers between devices  89.1 us (35%)
  starting transfers between devices  55.6 us (22%)
  Pallas kernels  42 us (17%)
  local copies, waits for them, and re-layouts  22.2 us (9%)
  blocking collectives  16.1 us (6%)
  between operations  14.2 us (6%)
  other arithmetic  11.5 us (5%)
    pallas_call x4, Pallas kernels, run_round(): pl.pallas_call(functools.partial(round_kernel, not carried, half_tiles),...  40.7 us
    ppermute x24, waiting for transfers between devices, shifted(): lax.ppermute(value, axes, [(a, (a + steps) % count) for a in range(count)])  34.8 us
    ppermute x24, starting transfers between devices, shifted(): lax.ppermute(value, axes, [(a, (a + steps) % count) for a in range(count)])  33.4 us
    all_to_all x1, waiting for transfers between devices, per_device(): pieces = lax.all_to_all(half, CHIPS, 0, 0, tiled=True)  26.9 us
    ppermute x4, waiting for transfers between devices, swap(): return lax.ppermute(value, axis, [(0, 1), (1, 0)])  23.3 us
    all_to_all x1, starting transfers between devices, per_device(): pieces = lax.all_to_all(half, CHIPS, 0, 0, tiled=True)  11 us
    unnamed x44, local copies, waits for them, and re-layouts  10.7 us
    all_gather x1, blocking collectives, per_device(): dst_parts.append(lax.all_gather(free_quarter, REP, axis=0, tiled=False))  8.77 us
  transfers between devices with their start and end apart: 30, of which 14 were waited for; matrix products, arithmetic and copies ran while one was open for 8% of the time, Pallas kernels for 8%

profile of v1, /device:TPU:32, one launch (start us, length us, event | category | flops | bytes accessed | tf_op | source)
XLA Modules:
  0.0 250.7 jit_solution(8198997405813827470)
XLA Ops:
  4.1 4.5 %collective-permute-start.5 = (bf16[200,128]{1,0:T(8,128)(2,1)}, bf16[200,128]{1,0:T(8,128)(2,1)S(1)}, u32[]{:S(2)}, u32[]{:S(2)}) collective-permute-start(bf16[200,128]{1,0:T(8,128)(2,1)} %param.9), channel_id=1, source_target_pairs={{0,12},{4,16},{8,20},{12,24},{16,28},{20,32},{24,36},{28,40},{32,4... | collective-permute-start | bytes 153608 | tf_op jit(solution)/shard_map/ppermute | solution.py:173
  8.6 7.3 %all-gather = bf16[800,128]{1,0:T(8,128)(2,1)S(1)} all-gather(bf16[200,128]{1,0:T(8,128)(2,1)} %param.9), channel_id=2, replica_groups=mesh['y'=4,'z'=8,'xl'=2,'xh'=2,'core'=2] {'xh','core'}, dimensions={0}, use_global_device_ids=true | all-gather | bytes 256000 | tf_op jit(solution)/shard_map/all_gather | solution.py:216
  15.9 3.2 %collective-permute-start.1 = (bf16[4,200,128]{2,1,0:T(8,128)(2,1)S(1)}, bf16[4,200,128]{2,1,0:T(8,128)(2,1)S(1)}, u32[]{:S(2)}, u32[]{:S(2)}) collective-permute-start(bf16[4,200,128]{2,1,0:T(8,128)(2,1)S(1)} %bitcast.65), channel_id=1, source_target_pairs={{0,128},{4,132},{8,136},{12,140},{16,144},{20,148},{24,152},{28,15... | collective-permute-start | bytes 614408 | tf_op jit(solution)/shard_map/ppermute | solution.py:173
  26.0 3.5 %collective-permute-start.6 = (bf16[200,128]{1,0:T(8,128)(2,1)S(1)}, bf16[200,128]{1,0:T(8,128)(2,1)S(1)}, u32[]{:S(2)}, u32[]{:S(2)}) collective-permute-start(bf16[200,128]{1,0:T(8,128)(2,1)S(1)} %select_select_fusion.4), channel_id=1, source_target_pairs={{0,16},{4,20},{8,24},{12,28},{16,32},{20,36},{24,40},{28,44},{32,4... | collective-permute-start | bytes 153608 | tf_op jit(solution)/shard_map/ppermute | solution.py:173
  31.0 4.2 %collective-permute-start.8 = (bf16[200,128]{1,0:T(8,128)(2,1)S(1)}, bf16[200,128]{1,0:T(8,128)(2,1)S(1)}, u32[]{:S(2)}, u32[]{:S(2)}) collective-permute-start(bf16[200,128]{1,0:T(8,128)(2,1)S(1)} %select_select_fusion.4), channel_id=1, source_target_pairs={{0,48},{4,52},{8,56},{12,60},{16,64},{20,68},{24,72},{28,76},{32,8... | collective-permute-start | bytes 153608 | tf_op jit(solution)/shard_map/ppermute | solution.py:173
  36.5 3.8 %collective-permute-done.7 = bf16[200,128]{1,0:T(8,128)(2,1)S(1)} collective-permute-done((bf16[200,128]{1,0:T(8,128)(2,1)S(1)}, bf16[200,128]{1,0:T(8,128)(2,1)S(1)}, u32[]{:S(2)}, u32[]{:S(2)}) %collective-permute-start.7) | collective-permute-done | bytes 51232 | tf_op jit(solution)/shard_map/ppermute | solution.py:173
  60.2 8.8 %all-gather.1 = bf16[800,128]{1,0:T(8,128)(2,1)S(1)} all-gather(bf16[200,128]{1,0:T(8,128)(2,1)S(1)} %select_select_fusion.2), channel_id=3, replica_groups=mesh['y'=4,'z'=8,'xl'=2,'xh'=2,'core'=2] {'xh','core'}, dimensions={0}, use_global_device_ids=true | all-gather | bytes 256000 | tf_op jit(solution)/shard_map/all_gather | solution.py:218
  72.0 9.5 %bucket_round.4 = (f32[4,200,128]{2,1,0:T(8,128)S(1)}, f32[2,2048,128]{2,1,0:T(8,128)S(1)}, f32[4,200,128]{2,1,0:T(8,128)S(1)}) custom-call(s32[5]{0:T(128)S(1)} %stack.63.meta, bf16[4,200,128]{2,1,0:T(8,128)(2,1)S(1)} %bitcast.67, bf16[4,200,128]{2,1,0:T(8,128)(2,1)S(1)} %collective-permute-done.dst_q, bf16[200,2176]{1,0:T(8,128)(2,1)S(1)} %copy-done, ...), custom_call_target="tpu_custom_call" | custom-call | tf_op jit(solution)/shard_map/bucket_round/pallas_call | solution.py:126
  82.8 10.5 %bucket_round.5 = (f32[4,200,128]{2,1,0:T(8,128)S(1)}, f32[2,2048,128]{2,1,0:T(8,128)S(1)}, f32[4,200,128]{2,1,0:T(8,128)S(1)}) custom-call(s32[5]{0:T(128)S(1)} %stack.67.meta, bf16[4,200,128]{2,1,0:T(8,128)(2,1)S(1)} %bitcast.68, bf16[4,200,128]{2,1,0:T(8,128)(2,1)S(1)} %collective-permute-done.1.dst_q, bf16[200,2176]{1,0:T(8,128)(2,1)S(1)} %copy-done, ...), custom_call_target="tpu_custom_call" | custom-call | tf_op jit(solution)/shard_map/bucket_round/pallas_call | solution.py:126
  94.7 10.5 %bucket_round.6 = (f32[4,200,128]{2,1,0:T(8,128)S(1)}, f32[2,2048,128]{2,1,0:T(8,128)S(1)}, f32[4,200,128]{2,1,0:T(8,128)S(1)}) custom-call(s32[5]{0:T(128)S(1)} %stack.71.meta, bf16[4,200,128]{2,1,0:T(8,128)(2,1)S(1)} %bitcast.69, bf16[4,200,128]{2,1,0:T(8,128)(2,1)S(1)} %collective-permute-done.2.dst_q, bf16[200,2176]{1,0:T(8,128)(2,1)S(1)} %copy-done, ...), custom_call_target="tpu_custom_call" | custom-call | tf_op jit(solution)/shard_map/bucket_round/pallas_call | solution.py:126
  107.2 10.3 %bucket_round.7 = (f32[4,200,128]{2,1,0:T(8,128)S(1)}, f32[2,2048,128]{2,1,0:T(8,128)S(1)}, f32[4,200,128]{2,1,0:T(8,128)S(1)}) custom-call(s32[5]{0:T(128)S(1)} %stack.75.meta, bf16[4,200,128]{2,1,0:T(8,128)(2,1)S(1)} %bitcast.70, bf16[4,200,128]{2,1,0:T(8,128)(2,1)S(1)} %bitcast.73, bf16[200,2176]{1,0:T(8,128)(2,1)S(1)} %copy-done, ...), custom_call_target="tpu_custom_call" | custom-call | tf_op jit(solution)/shard_map/bucket_round/pallas_call | solution.py:126
  120.1 3.0 %collective-permute-done.26 = f32[2048,128]{1,0:T(8,128)} collective-permute-done((f32[2048,128]{1,0:T(8,128)}, f32[2048,128]{1,0:T(8,128)}, u32[]{:S(2)}, u32[]{:S(2)}) %collective-permute-start.26) | collective-permute-done | bytes 1048608 | tf_op jit(solution)/shard_map/ppermute | solution.py:189
  125.5 11.0 %all-to-all-start = ((f32[128,16,128]{2,1,0:T(8,128)}), f32[128,16,128]{2,1,0:T(8,128)S(1)}, u32[]{:S(2)}, u32[]{:S(2)}) async-start(f32[128,16,128]{2,1,0:T(8,128)} %bitcast.79), calls=%async_computation | async-start | bytes 2097152 | tf_op jit(solution)/shard_map/all_to_all | solution.py:235
  139.2 26.9 %all-to-all-done = f32[128,16,128]{2,1,0:T(8,128)S(1)} async-done(((f32[128,16,128]{2,1,0:T(8,128)}), f32[128,16,128]{2,1,0:T(8,128)S(1)}, u32[]{:S(2)}, u32[]{:S(2)}) %all-to-all-start) | async-done | bytes 1048608 | tf_op jit(solution)/shard_map/all_to_all | solution.py:235
  167.3 8.1 %all-to-all-start.1 = ((f32[128,16,128]{2,1,0:T(8,128)}), f32[128,16,128]{2,1,0:T(8,128)S(1)}, u32[]{:S(2)}, u32[]{:S(2)}) async-start(f32[128,16,128]{2,1,0:T(8,128)} %tile.2), calls=%async_computation.1 | async-start | bytes 2097152 | tf_op jit(solution)/shard_map/all_to_all | solution.py:238
  177.1 3.1 %collective-permute-start.13 = (f32[5,200,128]{2,1,0:T(8,128)S(1)}, f32[5,200,128]{2,1,0:T(8,128)S(1)}, u32[]{:S(2)}, u32[]{:S(2)}) collective-permute-start(f32[5,200,128]{2,1,0:T(8,128)S(1)} %dynamic-slice_bitcast_fusion.2), channel_id=1, source_target_pairs={{0,2},{2,0},{1,3},{3,1},{4,6},{6,4},{5,7},{7,5},{8,10},{10,8},{9,1... | collective-permute-start | bytes 1536008 | tf_op jit(solution)/shard_map/ppermute | solution.py:189
  180.2 20.3 %collective-permute-done.13 = f32[5,200,128]{2,1,0:T(8,128)S(1)} collective-permute-done((f32[5,200,128]{2,1,0:T(8,128)S(1)}, f32[5,200,128]{2,1,0:T(8,128)S(1)}, u32[]{:S(2)}, u32[]{:S(2)}) %collective-permute-start.13) | collective-permute-done | bytes 512032 | tf_op jit(solution)/shard_map/ppermute | solution.py:189
  200.5 4.1 %all-to-all-done.1 = f32[128,16,128]{2,1,0:T(8,128)S(1)} async-done(((f32[128,16,128]{2,1,0:T(8,128)}), f32[128,16,128]{2,1,0:T(8,128)S(1)}, u32[]{:S(2)}, u32[]{:S(2)}) %all-to-all-start.1) | async-done | bytes 1048608 | tf_op jit(solution)/shard_map/all_to_all | solution.py:238
  206.0 2.6 %collective-permute-start.19 = (f32[200,128]{1,0:T(8,128)S(1)}, f32[200,128]{1,0:T(8,128)S(1)}, u32[]{:S(2)}, u32[]{:S(2)}) collective-permute-start(f32[200,128]{1,0:T(8,128)S(1)} %get-tuple-element.34), channel_id=1, source_target_pairs={{0,12},{4,16},{8,20},{12,24},{16,28},{20,32},{24,36},{28,40},{32,4... | collective-permute-start | bytes 307208 | tf_op jit(solution)/shard_map/ppermute | solution.py:173
  211.7 9.9 %collective-permute-done.19 = f32[200,128]{1,0:T(8,128)S(1)} collective-permute-done((f32[200,128]{1,0:T(8,128)S(1)}, f32[200,128]{1,0:T(8,128)S(1)}, u32[]{:S(2)}, u32[]{:S(2)}) %collective-permute-start.19) | collective-permute-done | bytes 102432 | tf_op jit(solution)/shard_map/ppermute | solution.py:173
  222.2 3.8 %collective-permute-start.22 = (f32[200,128]{1,0:T(8,128)S(1)}, f32[200,128]{1,0:T(8,128)}, u32[]{:S(2)}, u32[]{:S(2)}) collective-permute-start(f32[200,128]{1,0:T(8,128)S(1)} %select_select_fusion.1), channel_id=1, source_target_pairs={{0,48},{4,52},{8,56},{12,60},{16,64},{20,68},{24,72},{28,76},{32,8... | collective-permute-start | bytes 307208 | tf_op jit(solution)/shard_map/ppermute | solution.py:173
  226.7 10.2 %collective-permute-done.20 = f32[200,128]{1,0:T(8,128)S(1)} collective-permute-done((f32[200,128]{1,0:T(8,128)S(1)}, f32[200,128]{1,0:T(8,128)S(1)}, u32[]{:S(2)}, u32[]{:S(2)}) %collective-permute-start.20) | collective-permute-done | bytes 102432 | tf_op jit(solution)/shard_map/ppermute | solution.py:173
  241.5 2.4 collective-permute-done.15
  244.1 4.2 %collective-permute-done.23 = f32[200,128]{1,0:T(8,128)S(1)} collective-permute-done((f32[200,128]{1,0:T(8,128)S(1)}, f32[200,128]{1,0:T(8,128)S(1)}, u32[]{:S(2)}, u32[]{:S(2)}) %collective-permute-start.23) | collective-permute-done | bytes 102432 | tf_op jit(solution)/shard_map/ppermute | solution.py:173
  (114 shorter events, 51.2 us)
Async XLA Ops:
  0.7 25.2 %collective-permute-start.3 = (bf16[200,128]{1,0:T(8,128)(2,1)}, bf16[200,128]{1,0:T(8,128)(2,1)S(1)}, u32[]{:S(2)}, u32[]{:S(2)}) collective-permute-start(bf16[200,128]{1,0:T(8,128)(2,1)} %param.9), channel_id=1, source_target_pairs={{0,4},{4,8},{8,12},{12,16},{16,20},{20,24},{24,28},{28,32},{32,36}... | collective-permute-start | bytes 153608 | tf_op jit(solution)/shard_map/ppermute | solution.py:173
  2.2 23.7 %collective-permute-start.4 = (bf16[200,128]{1,0:T(8,128)(2,1)}, bf16[200,128]{1,0:T(8,128)(2,1)S(1)}, u32[]{:S(2)}, u32[]{:S(2)}) collective-permute-start(bf16[200,128]{1,0:T(8,128)(2,1)} %param.9), channel_id=1, source_target_pairs={{0,8},{4,12},{8,16},{12,20},{16,24},{20,28},{24,32},{28,36},{32,40... | collective-permute-start | bytes 153608 | tf_op jit(solution)/shard_map/ppermute | solution.py:173
  4.1 21.8 %collective-permute-start.5 = (bf16[200,128]{1,0:T(8,128)(2,1)}, bf16[200,128]{1,0:T(8,128)(2,1)S(1)}, u32[]{:S(2)}, u32[]{:S(2)}) collective-permute-start(bf16[200,128]{1,0:T(8,128)(2,1)} %param.9), channel_id=1, source_target_pairs={{0,12},{4,16},{8,20},{12,24},{16,28},{20,32},{24,36},{28,40},{32,4... | collective-permute-start | bytes 153608 | tf_op jit(solution)/shard_map/ppermute | solution.py:173
  15.9 53.1 %collective-permute-start = (bf16[4,200,128]{2,1,0:T(8,128)(2,1)S(1)}, bf16[4,200,128]{2,1,0:T(8,128)(2,1)S(1)}, u32[]{:S(2)}, u32[]{:S(2)}) collective-permute-start(bf16[4,200,128]{2,1,0:T(8,128)(2,1)S(1)} %bitcast.64), channel_id=1, source_target_pairs={{0,252},{4,0},{8,4},{12,8},{16,12},{20,16},{24,20},{28,24},{32,28}... | collective-permute-start | bytes 614408 | tf_op jit(solution)/shard_map/ppermute | solution.py:173
  15.9 66.9 %collective-permute-start.1 = (bf16[4,200,128]{2,1,0:T(8,128)(2,1)S(1)}, bf16[4,200,128]{2,1,0:T(8,128)(2,1)S(1)}, u32[]{:S(2)}, u32[]{:S(2)}) collective-permute-start(bf16[4,200,128]{2,1,0:T(8,128)(2,1)S(1)} %bitcast.65), channel_id=1, source_target_pairs={{0,128},{4,132},{8,136},{12,140},{16,144},{20,148},{24,152},{28,15... | collective-permute-start | bytes 614408 | tf_op jit(solution)/shard_map/ppermute | solution.py:173
  26.0 10.5 %collective-permute-start.6 = (bf16[200,128]{1,0:T(8,128)(2,1)S(1)}, bf16[200,128]{1,0:T(8,128)(2,1)S(1)}, u32[]{:S(2)}, u32[]{:S(2)}) collective-permute-start(bf16[200,128]{1,0:T(8,128)(2,1)S(1)} %select_select_fusion.4), channel_id=1, source_target_pairs={{0,16},{4,20},{8,24},{12,28},{16,32},{20,36},{24,40},{28,44},{32,4... | collective-permute-start | bytes 153608 | tf_op jit(solution)/shard_map/ppermute | solution.py:173
  29.4 10.9 %collective-permute-start.7 = (bf16[200,128]{1,0:T(8,128)(2,1)S(1)}, bf16[200,128]{1,0:T(8,128)(2,1)S(1)}, u32[]{:S(2)}, u32[]{:S(2)}) collective-permute-start(bf16[200,128]{1,0:T(8,128)(2,1)S(1)} %select_select_fusion.4), channel_id=1, source_target_pairs={{0,32},{4,36},{8,40},{12,44},{16,48},{20,52},{24,56},{28,60},{32,6... | collective-permute-start | bytes 153608 | tf_op jit(solution)/shard_map/ppermute | solution.py:173
  31.0 9.3 %collective-permute-start.8 = (bf16[200,128]{1,0:T(8,128)(2,1)S(1)}, bf16[200,128]{1,0:T(8,128)(2,1)S(1)}, u32[]{:S(2)}, u32[]{:S(2)}) collective-permute-start(bf16[200,128]{1,0:T(8,128)(2,1)S(1)} %select_select_fusion.4), channel_id=1, source_target_pairs={{0,48},{4,52},{8,56},{12,60},{16,64},{20,68},{24,72},{28,76},{32,8... | collective-permute-start | bytes 153608 | tf_op jit(solution)/shard_map/ppermute | solution.py:173
  40.4 18.7 %collective-permute-start.10 = (bf16[200,128]{1,0:T(8,128)(2,1)S(1)}, bf16[200,128]{1,0:T(8,128)(2,1)S(1)}, u32[]{:S(2)}, u32[]{:S(2)}) collective-permute-start(bf16[200,128]{1,0:T(8,128)(2,1)S(1)} %select_select_fusion.3), channel_id=1, source_target_pairs={{0,128},{4,132},{8,136},{12,140},{16,144},{20,148},{24,152},{28,15... | collective-permute-start | bytes 153608 | tf_op jit(solution)/shard_map/ppermute | solution.py:173
  40.5 19.7 %collective-permute-start.11 = (bf16[200,128]{1,0:T(8,128)(2,1)S(1)}, bf16[200,128]{1,0:T(8,128)(2,1)S(1)}, u32[]{:S(2)}, u32[]{:S(2)}) collective-permute-start(bf16[200,128]{1,0:T(8,128)(2,1)S(1)} %select_select_fusion.3), channel_id=1, source_target_pairs={{0,192},{4,196},{8,200},{12,204},{16,208},{20,212},{24,216},{28,22... | collective-permute-start | bytes 153608 | tf_op jit(solution)/shard_map/ppermute | solution.py:173
  42.5 17.7 %collective-permute-start.9 = (bf16[200,128]{1,0:T(8,128)(2,1)S(1)}, bf16[200,128]{1,0:T(8,128)(2,1)S(1)}, u32[]{:S(2)}, u32[]{:S(2)}) collective-permute-start(bf16[200,128]{1,0:T(8,128)(2,1)S(1)} %select_select_fusion.3), channel_id=1, source_target_pairs={{0,64},{4,68},{8,72},{12,76},{16,80},{20,84},{24,88},{28,92},{32,9... | collective-permute-start | bytes 153608 | tf_op jit(solution)/shard_map/ppermute | solution.py:173
  59.1 35.6 %collective-permute-start.2 = (bf16[4,200,128]{2,1,0:T(8,128)(2,1)S(1)}, bf16[4,200,128]{2,1,0:T(8,128)(2,1)S(1)}, u32[]{:S(2)}, u32[]{:S(2)}) collective-permute-start(bf16[4,200,128]{2,1,0:T(8,128)(2,1)S(1)} %bitcast.66), channel_id=1, source_target_pairs={{0,4},{4,8},{8,12},{12,16},{16,20},{20,24},{24,28},{28,32},{32,36}... | collective-permute-start | bytes 614408 | tf_op jit(solution)/shard_map/ppermute | solution.py:173
  125.5 40.6 %all-to-all-start = ((f32[128,16,128]{2,1,0:T(8,128)}), f32[128,16,128]{2,1,0:T(8,128)S(1)}, u32[]{:S(2)}, u32[]{:S(2)}) async-start(f32[128,16,128]{2,1,0:T(8,128)} %bitcast.79), calls=%async_computation | async-start | bytes 2097152 | tf_op jit(solution)/shard_map/all_to_all | solution.py:235
  139.2 36.2 %collective-permute-start.12 = (f32[5,2,200,128]{3,2,1,0:T(8,128)}, f32[5,2,200,128]{3,2,1,0:T(8,128)}, u32[]{:S(2)}, u32[]{:S(2)}) collective-permute-start(f32[5,2,200,128]{3,2,1,0:T(8,128)} %dynamic-slice_bitcast_fusion.1), channel_id=1, source_target_pairs={{0,1},{1,0},{2,3},{3,2},{4,5},{5,4},{6,7},{7,6},{8,9},{9,8},{10,11... | collective-permute-start | bytes 3072008 | tf_op jit(solution)/shard_map/ppermute | solution.py:189
  167.3 37.3 %all-to-all-start.1 = ((f32[128,16,128]{2,1,0:T(8,128)}), f32[128,16,128]{2,1,0:T(8,128)S(1)}, u32[]{:S(2)}, u32[]{:S(2)}) async-start(f32[128,16,128]{2,1,0:T(8,128)} %tile.2), calls=%async_computation.1 | async-start | bytes 2097152 | tf_op jit(solution)/shard_map/all_to_all | solution.py:238
  177.1 23.3 %collective-permute-start.13 = (f32[5,200,128]{2,1,0:T(8,128)S(1)}, f32[5,200,128]{2,1,0:T(8,128)S(1)}, u32[]{:S(2)}, u32[]{:S(2)}) collective-permute-start(f32[5,200,128]{2,1,0:T(8,128)S(1)} %dynamic-slice_bitcast_fusion.2), channel_id=1, source_target_pairs={{0,2},{2,0},{1,3},{3,1},{4,6},{6,4},{5,7},{7,5},{8,10},{10,8},{9,1... | collective-permute-start | bytes 1536008 | tf_op jit(solution)/shard_map/ppermute | solution.py:189
  204.6 44.8 %collective-permute-start.27 = (f32[2048,128]{1,0:T(8,128)S(1)}, f32[2048,128]{1,0:T(8,128)S(1)}, u32[]{:S(2)}, u32[]{:S(2)}) collective-permute-start(f32[2048,128]{1,0:T(8,128)S(1)} %bitcast.71), channel_id=1, source_target_pairs={{0,1},{1,0},{2,3},{3,2},{4,5},{5,4},{6,7},{7,6},{8,9},{9,8},{10,11... | collective-permute-start | bytes 3145736 | tf_op jit(solution)/shard_map/ppermute | solution.py:189
  206.0 15.6 %collective-permute-start.19 = (f32[200,128]{1,0:T(8,128)S(1)}, f32[200,128]{1,0:T(8,128)S(1)}, u32[]{:S(2)}, u32[]{:S(2)}) collective-permute-start(f32[200,128]{1,0:T(8,128)S(1)} %get-tuple-element.34), channel_id=1, source_target_pairs={{0,12},{4,16},{8,20},{12,24},{16,28},{20,32},{24,36},{28,40},{32,4... | collective-permute-start | bytes 307208 | tf_op jit(solution)/shard_map/ppermute | solution.py:173
  221.7 15.2 %collective-permute-start.20 = (f32[200,128]{1,0:T(8,128)S(1)}, f32[200,128]{1,0:T(8,128)S(1)}, u32[]{:S(2)}, u32[]{:S(2)}) collective-permute-start(f32[200,128]{1,0:T(8,128)S(1)} %select_select_fusion.1), channel_id=1, source_target_pairs={{0,16},{4,20},{8,24},{12,28},{16,32},{20,36},{24,40},{28,44},{32,4... | collective-permute-start | bytes 307208 | tf_op jit(solution)/shard_map/ppermute | solution.py:173
  221.8 16.3 %collective-permute-start.21 = (f32[200,128]{1,0:T(8,128)S(1)}, f32[200,128]{1,0:T(8,128)}, u32[]{:S(2)}, u32[]{:S(2)}) collective-permute-start(f32[200,128]{1,0:T(8,128)S(1)} %select_select_fusion.1), channel_id=1, source_target_pairs={{0,32},{4,36},{8,40},{12,44},{16,48},{20,52},{24,56},{28,60},{32,6... | collective-permute-start | bytes 307208 | tf_op jit(solution)/shard_map/ppermute | solution.py:173
  222.2 17.1 %collective-permute-start.22 = (f32[200,128]{1,0:T(8,128)S(1)}, f32[200,128]{1,0:T(8,128)}, u32[]{:S(2)}, u32[]{:S(2)}) collective-permute-start(f32[200,128]{1,0:T(8,128)S(1)} %select_select_fusion.1), channel_id=1, source_target_pairs={{0,48},{4,52},{8,56},{12,60},{16,64},{20,68},{24,72},{28,76},{32,8... | collective-permute-start | bytes 307208 | tf_op jit(solution)/shard_map/ppermute | solution.py:173
  226.6 13.8 %collective-permute-start.14 = (f32[200,128]{1,0:T(8,128)S(1)}, f32[200,128]{1,0:T(8,128)S(1)}, u32[]{:S(2)}, u32[]{:S(2)}) collective-permute-start(f32[200,128]{1,0:T(8,128)S(1)} %get-tuple-element.37), channel_id=1, source_target_pairs={{0,4},{4,8},{8,12},{12,16},{16,20},{20,24},{24,28},{28,32},{32,36}... | collective-permute-start | bytes 307208 | tf_op jit(solution)/shard_map/ppermute | solution.py:173
  240.3 8.0 %collective-permute-start.23 = (f32[200,128]{1,0:T(8,128)S(1)}, f32[200,128]{1,0:T(8,128)S(1)}, u32[]{:S(2)}, u32[]{:S(2)}) collective-permute-start(f32[200,128]{1,0:T(8,128)S(1)} %select_select_fusion), channel_id=1, source_target_pairs={{0,64},{4,68},{8,72},{12,76},{16,80},{20,84},{24,88},{28,92},{32,9... | collective-permute-start | bytes 307208 | tf_op jit(solution)/shard_map/ppermute | solution.py:173
  240.4 7.9 %collective-permute-start.24 = (f32[200,128]{1,0:T(8,128)S(1)}, f32[200,128]{1,0:T(8,128)S(1)}, u32[]{:S(2)}, u32[]{:S(2)}) collective-permute-start(f32[200,128]{1,0:T(8,128)S(1)} %select_select_fusion), channel_id=1, source_target_pairs={{0,128},{4,132},{8,136},{12,140},{16,144},{20,148},{24,152},{28,15... | collective-permute-start | bytes 307208 | tf_op jit(solution)/shard_map/ppermute | solution.py:173
  (26 other events, 280.5 us)
